TPU v7x, 256 devices: a whole 4x4x8 slice. The times are simulated.
256 devices in a mesh: seq: 64 (over z_lo, x, y, core), tp: 4 (over z_hi).
Axes of the slice: x: 4, y: 4, z: 8 (z_hi: 4, z_lo: 2; z = z_hi * 2 + z_lo), core: 2. Of those that a mesh axis runs over, the one named last changes fastest.
Arguments:
- code_ids: int32 [4, 8192], P(None, 'seq'), may hold values from 0 to 1023
- delays: int32 [4], replicated, may hold values from 0 to 3, as said below
- embed_table: bfloat16 [4, 1024, 2048], P(None, None, 'tp'), may hold values from -2.5 to 2.5
- project_in: bfloat16 [2048, 3, 2048], P(None, None, 'tp'), may hold values from -8 to 8
- project_out: bfloat16 [2048, 2048], P('tp'), may hold values from -0.125 to 0.125
- grad_output: bfloat16 [8192, 2048], P('seq', 'tp'), may hold values from -6 to 6
Outputs:
- layer_output: bfloat16 [8192, 2048], P('seq', 'tp')
- grad_embed: float32 [8192, 2048], P('seq', 'tp')
- grad_project_out: float32 [2048, 2048], P('tp', 'seq')
Inputs may be any that keep to these rules, and one draw needn't show every extreme that they name: `delays`: at least one codebook has exactly 3.
All inputs are finite; a program needn't handle non-finite values.
Results may differ from a plain program's by a relative error of at most 0.035.
Values may be sent and summed in bfloat16 or wider, within the bound.
No kernel may reach another device: no remote copies, remote signals or barrier semaphores. Data moves between devices by JAX's collectives and lax.ppermute only.
A program may use at most 128 MiB of HBM per device.

v0:
```python
import math

import jax
import jax.numpy as jnp
from jax import lax
from jax.sharding import PartitionSpec as P

HD = 64
BOOKS = 4
DMAX = 3


NEGATIVE = -1e30


def from_behind(block, axis, distance):
    devices = range(lax.axis_size(axis))
    route = [(i - distance, i) for i in devices if i - distance in devices]
    return lax.ppermute(block, axis, route)


def contract(left_side, right_side, left_axis, right_axis):
    return lax.dot_general(
        left_side,
        right_side,
        (((left_axis,), (right_axis,)), ((), ())),
        preferred_element_type=jnp.float32,
    )


def to_heads(blocks, groups):
    tok_rows, head_count, feature_width = blocks.shape
    sub_rows = tok_rows // groups
    arranged = blocks.reshape(groups, sub_rows, head_count, feature_width).transpose(2, 0, 1, 3)
    return arranged.reshape(head_count * groups, sub_rows * feature_width)


def from_heads(slot_rows, groups, head_count, feature_width):
    sub_rows = slot_rows.shape[1] // feature_width
    arranged = slot_rows.reshape(head_count, groups, sub_rows, feature_width).transpose(1, 2, 0, 3)
    return arranged.reshape(groups * sub_rows, head_count, feature_width)


def copies(blocks, groups):
    tok_rows, head_count, feature_width = blocks.shape
    spread = jnp.broadcast_to(
        blocks.transpose(1, 0, 2)[:, None], (head_count, groups, tok_rows, feature_width)
    )
    return spread.reshape(head_count * groups, tok_rows * feature_width)


def attend(queries, key_rows, value_rows, query_pos, scaling, block_size):
    query_count = queries.shape[0]
    block_count = key_rows.shape[0] // block_size
    key_blocks = key_rows.reshape(block_count, block_size, key_rows.shape[1])
    value_blocks = value_rows.reshape(block_count, block_size, value_rows.shape[1])
    starts = jnp.arange(block_count, dtype=jnp.int32) * block_size

    def attend_visit_block(carried, inputs):
        running_top, running_total, running_sum = carried
        key_block, value_block, first_key = inputs
        scores = contract(queries, key_block, 1, 1) * scaling
        allowed = (first_key + jnp.arange(block_size, dtype=jnp.int32))[None, :] <= query_pos[
            :, None
        ]
        scores = jnp.where(allowed, scores, NEGATIVE)
        new_top = jnp.maximum(running_top, jnp.max(scores, axis=1))
        weights = jnp.where(allowed, jnp.exp(scores - new_top[:, None]), 0.0)
        factor = jnp.exp(running_top - new_top)
        running_total = running_total * factor + jnp.sum(weights, axis=1)
        running_sum = running_sum * factor[:, None] + jnp.dot(
            weights.astype(jnp.bfloat16), value_block, preferred_element_type=jnp.float32
        )
        return ((new_top, running_total, running_sum), None)

    initial = (
        jnp.full((query_count,), NEGATIVE, jnp.float32),
        jnp.zeros((query_count,), jnp.float32),
        jnp.zeros((query_count, value_rows.shape[1]), jnp.float32),
    )
    finals, unused_out = lax.scan(attend_visit_block, initial, (key_blocks, value_blocks, starts))
    final_top, final_total, final_sum = finals
    return (
        (final_sum / final_total[:, None]).astype(jnp.bfloat16),
        final_top + jnp.log(final_total),
    )


def query_side(
    queries, grad_rows, log_total, deltas, key_rows, value_rows, query_pos, scaling, block_size
):
    block_count = key_rows.shape[0] // block_size
    key_blocks = key_rows.reshape(block_count, block_size, key_rows.shape[1])
    value_blocks = value_rows.reshape(block_count, block_size, value_rows.shape[1])
    starts = jnp.arange(block_count, dtype=jnp.int32) * block_size

    def query_visit_block(grad_query, inputs):
        key_block, value_block, first_key = inputs
        scores = contract(queries, key_block, 1, 1) * scaling
        allowed = (first_key + jnp.arange(block_size, dtype=jnp.int32))[None, :] <= query_pos[
            :, None
        ]
        chances = jnp.where(allowed, jnp.exp(scores - log_total[:, None]), 0.0)
        prob_grad = contract(grad_rows, value_block, 1, 1)
        score_grad = (chances * (prob_grad - deltas[:, None]) * scaling).astype(jnp.bfloat16)
        grad_query = grad_query + jnp.dot(score_grad, key_block, preferred_element_type=jnp.float32)
        value_grad = contract(chances.astype(jnp.bfloat16), grad_rows, 0, 0)
        key_grad = contract(score_grad, queries, 0, 0)
        return (grad_query, (key_grad, value_grad))

    initial = jnp.zeros(queries.shape, jnp.float32)
    return lax.scan(query_visit_block, initial, (key_blocks, value_blocks, starts))


def body(code_ids, delays, embed_table, project_in, project_out, grad_output):
    tok_rows = code_ids.shape[1]
    seq_count = lax.axis_size("seq")
    seq_index = lax.axis_index("seq")
    local_heads = project_in.shape[2] // HD
    group_size = seq_count // local_heads
    sub_rows = tok_rows // group_size
    total_rows = tok_rows * seq_count
    block_size = math.gcd(total_rows, 1024)
    scaling = HD ** (-0.5)
    subset = seq_index % group_size
    tail_ids = code_ids[:, tok_rows - DMAX :]
    before = from_behind(tail_ids, "seq", 1)
    joined = jnp.concatenate([before, code_ids], axis=1)
    local_pos = jnp.arange(tok_rows, dtype=jnp.int32)
    lookup = DMAX + local_pos[None, :] - delays[:, None]
    picked = jnp.take_along_axis(joined, lookup, axis=1)
    usable = (seq_index * tok_rows + local_pos)[None, :] >= delays[:, None]
    embedded = jnp.zeros((tok_rows, embed_table.shape[2]), jnp.float32)
    for codebook in range(BOOKS):
        looked = jnp.take(embed_table[codebook], picked[codebook], axis=0).astype(jnp.float32)
        embedded = embedded + jnp.where(usable[codebook][:, None], looked, 0.0)
    summed = embedded.astype(jnp.bfloat16)
    summed_full, grad_full = (
        lax.all_gather(summed, "tp", axis=1, tiled=True),
        lax.all_gather(grad_output, "tp", axis=1, tiled=True),
    )
    features = summed_full.astype(jnp.float32)
    inv_rms = lax.rsqrt(jnp.mean(features * features, axis=1) + 1e-05)
    normed = features * inv_rms[:, None]
    flat_in = project_in.reshape(project_in.shape[0], 3 * local_heads * HD)
    projected = jnp.dot(
        normed.astype(jnp.bfloat16), flat_in, preferred_element_type=jnp.float32
    ).astype(jnp.bfloat16)
    projected = projected.reshape(tok_rows, 3, local_heads, HD)
    query_local = projected[:, 0]
    key_value = jnp.concatenate([projected[:, 1], projected[:, 2]], axis=2)
    query_slots, pair_slots = (
        lax.all_to_all(
            to_heads(query_local, group_size), "seq", split_axis=0, concat_axis=0, tiled=True
        ),
        lax.all_to_all(
            copies(key_value, group_size), "seq", split_axis=0, concat_axis=0, tiled=True
        ),
    )
    queries = query_slots.reshape(seq_count * sub_rows, HD)
    pair_rows = pair_slots.reshape(total_rows, 2 * HD)
    key_rows = pair_rows[:, :HD]
    value_rows = pair_rows[:, HD:]
    query_pos = (
        jnp.arange(seq_count, dtype=jnp.int32)[:, None] * tok_rows
        + subset * sub_rows
        + jnp.arange(sub_rows, dtype=jnp.int32)[None, :]
    ).reshape(-1)
    attended, log_total = attend(queries, key_rows, value_rows, query_pos, scaling, block_size)
    back_slots = lax.all_to_all(
        attended.reshape(seq_count, sub_rows * HD), "seq", split_axis=0, concat_axis=0, tiled=True
    )
    attention_heads = from_heads(back_slots, group_size, local_heads, HD)
    attention = attention_heads.reshape(tok_rows, local_heads * HD)
    projection = jnp.dot(attention, project_out, preferred_element_type=jnp.float32)
    proj_share = lax.psum_scatter(
        projection.astype(jnp.bfloat16), "tp", scatter_dimension=1, tiled=True
    ).astype(jnp.float32)
    layer_output = (summed.astype(jnp.float32) + proj_share).astype(jnp.bfloat16)
    grad_project_out = lax.psum_scatter(
        contract(attention, grad_full, 0, 0), "seq", scatter_dimension=1, tiled=True
    )
    grad_attention = contract(grad_full, project_out, 1, 1).astype(jnp.bfloat16)
    grad_heads = grad_attention.reshape(tok_rows, local_heads, HD)
    grad_slots = lax.all_to_all(
        to_heads(grad_heads, group_size), "seq", split_axis=0, concat_axis=0, tiled=True
    )
    grad_rows = grad_slots.reshape(seq_count * sub_rows, HD)
    deltas = jnp.sum(grad_rows.astype(jnp.float32) * attended.astype(jnp.float32), axis=1)
    grad_query, key_parts = query_side(
        queries, grad_rows, log_total, deltas, key_rows, value_rows, query_pos, scaling, block_size
    )
    key_grad = key_parts[0].reshape(total_rows, HD)
    value_grad = key_parts[1].reshape(total_rows, HD)
    pair_grad = jnp.concatenate([key_grad, value_grad], axis=1).reshape(
        seq_count, tok_rows * 2 * HD
    )
    query_back, pair_back = (
        lax.all_to_all(
            grad_query.reshape(seq_count, sub_rows * HD).astype(jnp.bfloat16),
            "seq",
            split_axis=0,
            concat_axis=0,
            tiled=True,
        ).astype(jnp.float32),
        lax.all_to_all(
            pair_grad.astype(jnp.bfloat16), "seq", split_axis=0, concat_axis=0, tiled=True
        ).astype(pair_grad.dtype),
    )
    query_grads = from_heads(query_back, group_size, local_heads, HD)
    pair_grads = jnp.sum(
        pair_back.reshape(local_heads, group_size, tok_rows, 2 * HD), axis=1
    ).transpose(1, 0, 2)
    key_grads = pair_grads[:, :, :HD]
    value_grads = pair_grads[:, :, HD:]
    grad_triple = (
        jnp.stack([query_grads, key_grads, value_grads], axis=1)
        .astype(jnp.bfloat16)
        .reshape(tok_rows, 3 * local_heads * HD)
    )
    grad_normed = contract(grad_triple, flat_in, 1, 1)
    width_local = grad_output.shape[1]
    tp_start = lax.axis_index("tp") * width_local
    grad_total = lax.psum(grad_normed.astype(jnp.bfloat16), "tp").astype(jnp.float32)
    centre = jnp.mean(grad_total * normed, axis=1)
    grad_whole = inv_rms[:, None] * (grad_total - normed * centre[:, None])
    grad_embed = grad_output.astype(jnp.float32) + lax.dynamic_slice_in_dim(
        grad_whole, tp_start, width_local, 1
    )
    return (layer_output, grad_embed, grad_project_out)


def solution(mesh):
    placed = (
        P(None, "seq"),
        P(),
        P(None, None, "tp"),
        P(None, None, "tp"),
        P("tp", None),
        P("seq", "tp"),
    )
    return jax.shard_map(
        body,
        mesh=mesh,
        in_specs=placed,
        out_specs=(P("seq", "tp"), P("seq", "tp"), P("tp", "seq")),
        check_vma=False,
    )
```

profile of v0, /device:TPU:64, one launch (start us, length us, event | category | flops | bytes accessed | tf_op | source)
XLA Modules:
  0.0 846.3 jit_solution(4287675573347037496)
XLA Ops:
  9.8 18.3 %all_gather.7 = bf16[128,2048]{1,0:T(8,128)(2,1)S(1)} all-gather(bf16[128,512]{1,0:T(8,128)(2,1)} %param.17), channel_id=1, replica_groups=mesh['seq'=64,'tp'=4] {'tp'}, dimensions={1}, use_global_device_ids=true | all-gather | bytes 655360 | tf_op jit(solution)/shard_map/all_gather | solution.py:140
  32.8 9.7 %all-to-all-start.3 = ((bf16[64,2,512]{2,1,0:T(2,128)(2,1)}), bf16[64,2,512]{2,1,0:T(2,128)(2,1)}, u32[]{:S(2)}, u32[]{:S(2)}) async-start(bf16[64,2,512]{2,1,0:T(2,128)(2,1)} %reshape.298), calls=%async_computation.4 | async-start | bytes 262144 | tf_op jit(solution)/shard_map/all_to_all | solution.py:185
  43.3 4.0 slice_bitcast_fusion.3
  47.3 8.8 %copy.74 = bf16[2048,3,512]{0,2,1:T(8,128)(2,1)} copy(bf16[2048,3,512]{2,0,1:T(8,128)(2,1)} %param.15) | data formatting | bytes 12582912 | tf_op args[3]
  56.2 4.8 gather_fusion
  61.7 2.2 gather_fusion.1
  63.9 2.2 gather_fusion.2
  66.2 2.2 gather_fusion.4
  71.1 14.9 %all_gather.6 = bf16[128,2048]{1,0:T(8,128)(2,1)S(1)} all-gather(bf16[128,512]{1,0:T(8,128)(2,1)S(1)} %add_convert_fusion.1), channel_id=1, replica_groups=mesh['seq'=64,'tp'=4] {'tp'}, dimensions={1}, use_global_device_ids=true | all-gather | bytes 655360 | tf_op jit(solution)/shard_map/all_gather | solution.py:139
  86.2 5.0 convolution_convert_fusion.2
  94.6 10.4 %all-to-all-start.1 = ((bf16[64,2,512]{2,1,0:T(2,128)(2,1)}), bf16[64,2,512]{2,1,0:T(2,128)(2,1)S(1)}, u32[]{:S(2)}, u32[]{:S(2)}) async-start(bf16[64,2,512]{2,1,0:T(2,128)(2,1)} %reshape.294), calls=%async_computation.1 | async-start | bytes 262144 | tf_op jit(solution)/shard_map/all_to_all | solution.py:153
  108.0 10.0 %all_to_all.42 = bf16[64,1,16384]{2,1,0:T(2,128)(2,1)} reshape(bf16[8,8,128,128]{3,2,1,0:T(8,128)(2,1)} %broadcast_in_dim.108) | data formatting | bytes 4194304 | tf_op jit(solution)/shard_map/all_to_all | solution.py:156
  118.1 14.4 %reduce.6 = bf16[64,16384]{1,0:T(8,128)(2,1)} reduce(bf16[64,1,16384]{2,1,0:T(2,128)(2,1)} %all_to_all.42, bf16[]{:T(256)} %broadcast.228), dimensions={1}, to_apply=%all_to_all.42.reduce_sub_computation | reduce | bytes 4194306 | tf_op jit(solution)/shard_map/all_to_all | solution.py:156
  132.5 4.5 reshape.292
  137.0 9.3 %all-to-all-start = ((bf16[64,2,8192]{2,1,0:T(2,128)(2,1)}), bf16[64,2,8192]{2,1,0:T(2,128)(2,1)}, u32[]{:S(2)}, u32[]{:S(2)}) async-start(bf16[64,2,8192]{2,1,0:T(2,128)(2,1)} %reshape.292), calls=%async_computation | async-start | bytes 4194304 | tf_op jit(solution)/shard_map/all_to_all | solution.py:156
  154.2 20.4 %all-to-all-done = bf16[64,2,8192]{2,1,0:T(2,128)(2,1)} async-done(((bf16[64,2,8192]{2,1,0:T(2,128)(2,1)}), bf16[64,2,8192]{2,1,0:T(2,128)(2,1)}, u32[]{:S(2)}, u32[]{:S(2)}) %all-to-all-start) | async-done | bytes 2097184 | tf_op jit(solution)/shard_map/all_to_all | solution.py:156
  174.7 10.5 %reshape.293 = bf16[64,1,16384]{2,1,0:T(2,128)(2,1)} reshape(bf16[64,2,8192]{2,1,0:T(2,128)(2,1)} %all-to-all-done) | data formatting | bytes 4194304
  185.1 13.9 %reduce = bf16[64,16384]{1,0:T(8,128)(2,1)} reduce(bf16[64,1,16384]{2,1,0:T(2,128)(2,1)} %reshape.293, bf16[]{:T(256)} %constant.117), dimensions={1}, to_apply=%all_to_all.33.reduce_sub_computation | reduce | bytes 4194306 | tf_op jit(solution)/shard_map/all_to_all | solution.py:156
  199.0 4.2 reshape.228
  203.2 5.0 fusion.58
  208.2 60.8 %while.30 = (s32[]{:T(128)}, f32[1024]{0:T(1024)S(1)}, f32[1024]{0:T(1024)S(1)}, f32[1024,64]{0,1:T(8,128)}, s32[8]{0:T(128)S(1)}, /*index=5*/bf16[8,1024,64]{2,...) while((s32[]{:T(128)}, f32[1024]{0:T(1024)S(1)}, ...), condition=%wide.region_4.6_spmd.clone, body=%wide.region_1.5_spmd.clone.sunk | while | flops 285416448 | bytes 15966673 | solution.py:81
  272.9 81.0 %while.31 = (s32[]{:T(128)}, f32[1024,64]{0,1:T(8,128)S(1)}, bf16[8,1024,64]{1,2,0:T(8,128)(2,1)}, bf16[8,1024,64]{1,2,0:T(8,128)(2,1)}, s32[8]{0:T(128)S(1)}, /...) while((s32[]{:T(128)}, f32[1024,64]{0,1:T(8,128)S(1)}, ...), condition=%wide.region_8.10_spmd.clone, body=%wide.region_7.9_spmd.clone.sunk | while | flops 684853248 | bytes 21279164 | solution.py:112
  277.8 2.4 fusion.116
  287.9 2.4 fusion.116
  298.0 2.4 fusion.116
  308.1 2.4 fusion.116
  318.2 2.4 fusion.116
  328.3 2.4 fusion.116
  338.4 2.4 fusion.116
  348.5 2.4 fusion.116
  356.3 6.5 all-to-all-start.4
  362.8 2.4 copy.97
  367.4 2.3 copy.96
  371.2 7.4 all-to-all-start.2
  378.7 3.1 pad_maximum_fusion
  381.7 4.1 copy.90
  385.8 10.0 %convert_element_type.148 = bf16[64,1,16384]{2,1,0:T(2,128)(2,1)} reshape(bf16[8192,128]{1,0:T(8,128)(2,1)} %copy.90) | data formatting | bytes 4194304 | tf_op jit(solution)/shard_map/convert_element_type | solution.py:207
  395.8 14.4 %reduce.9 = bf16[64,16384]{1,0:T(8,128)(2,1)} reduce(bf16[64,1,16384]{2,1,0:T(2,128)(2,1)} %convert_element_type.148, bf16[]{:T(256)} %broadcast.228), dimensions={1}, to_apply=%convert_element_type.148.reduce_sub_computation | reduce | bytes 4194306 | tf_op jit(solution)/shard_map/convert_element_type | solution.py:207
  410.3 4.5 reshape.300
  414.8 9.2 %all-to-all-start.5 = ((bf16[64,2,8192]{2,1,0:T(2,128)(2,1)}), bf16[64,2,8192]{2,1,0:T(2,128)(2,1)}, u32[]{:S(2)}, u32[]{:S(2)}) async-start(bf16[64,2,8192]{2,1,0:T(2,128)(2,1)} %reshape.300), calls=%async_computation.6 | async-start | bytes 4194304 | tf_op jit(solution)/shard_map/all_to_all | solution.py:206
  428.0 31.4 %all-to-all-done.5 = bf16[64,2,8192]{2,1,0:T(2,128)(2,1)} async-done(((bf16[64,2,8192]{2,1,0:T(2,128)(2,1)}), bf16[64,2,8192]{2,1,0:T(2,128)(2,1)}, u32[]{:S(2)}, u32[]{:S(2)}) %all-to-all-start.5) | async-done | bytes 2097184 | tf_op jit(solution)/shard_map/all_to_all | solution.py:206
  459.5 10.5 %reshape.301 = bf16[64,1,16384]{2,1,0:T(2,128)(2,1)} reshape(bf16[64,2,8192]{2,1,0:T(2,128)(2,1)} %all-to-all-done.5) | data formatting | bytes 4194304
  469.9 11.8 %convert_element_type.143 = f32[64,1,16384]{2,1,0:T(1,128)} convert(bf16[64,1,16384]{2,1,0:T(2,128)(2,1)} %reshape.301) | non-fusion elementwise | flops 1048576 | bytes 6291456 | tf_op jit(solution)/shard_map/convert_element_type | solution.py:208
  481.7 2.5 reduce_sum.47
  487.7 4.8 convolution_convert_fusion
  492.6 2.7 fusion.60
  496.9 47.8 %all-reduce.2.cloned.1.call-done = bf16[128,2048]{1,0:T(8,128)(2,1)} async-done(((bf16[128,2048]{1,0:T(8,128)(2,1)}), bf16[128,2048]{1,0:T(8,128)(2,1)}) %all-reduce.2.cloned.1.call-update) | async-done | bytes 524304 | tf_op jit(solution)/shard_map/psum | solution.py:224
  548.1 291.4 %reduce-scatter.5.cloned.1.call-done = f32[512,32]{0,1:T(8,128)} async-done(((f32[512,2048]{0,1:T(8,128)}), f32[512,32]{0,1:T(8,128)}) %reduce-scatter.5.cloned.1.call-update) | async-done | bytes 65552 | tf_op jit(solution)/shard_map/reduce_scatter | solution.py:180
  (282 shorter events, 169.8 us)
Async XLA Ops:
  7.2 21.7 %copy-start = (bf16[512,2048]{1,0:T(8,128)(2,1)S(1)}, bf16[512,2048]{1,0:T(8,128)(2,1)}, u32[]{:S(2)}) copy-start(bf16[512,2048]{1,0:T(8,128)(2,1)} %param.16) | copy-start | bytes 6291460
  7.2 35.4 %copy-start.11 = (s32[4]{0:T(128)S(1)}, s32[4]{0:T(128)}, u32[]{:S(2)}) copy-start(s32[4]{0:T(128)} %param.13) | copy-start | bytes 52
  8.1 48.0 %collective-permute-start = (s32[4,3]{1,0:T(4,128)S(1)}, s32[4,3]{1,0:T(4,128)S(1)}, u32[]{:S(2)}, u32[]{:S(2)}) collective-permute-start(s32[4,3]{1,0:T(4,128)S(1)} %slice.64), channel_id=1, source_target_pairs={{0,4},{4,8},{8,12},{12,16},{16,20},{20,24},{24,28},{28,32},{32,36}... | collective-permute-start | bytes 152 | tf_op jit(solution)/shard_map/ppermute | solution.py:19
  28.1 0.8 copy-start.1
  32.8 61.8 %all-to-all-start.3 = ((bf16[64,2,512]{2,1,0:T(2,128)(2,1)}), bf16[64,2,512]{2,1,0:T(2,128)(2,1)}, u32[]{:S(2)}, u32[]{:S(2)}) async-start(bf16[64,2,512]{2,1,0:T(2,128)(2,1)} %reshape.298), calls=%async_computation.4 | async-start | bytes 262144 | tf_op jit(solution)/shard_map/all_to_all | solution.py:185
  47.3 8.8 %copy-start.10 = (s32[4,128]{1,0:T(4,128)S(1)}, s32[4,128]{1,0:T(4,128)}, u32[]{:S(2)}) copy-start(s32[4,128]{1,0:T(4,128)} %param.12) | copy-start | bytes 6148
  71.1 15.1 %copy-start.3 = (bf16[128,512]{1,0:T(8,128)(2,1)}, bf16[128,512]{1,0:T(8,128)(2,1)S(1)}, u32[]{:S(2)}) copy-start(bf16[128,512]{1,0:T(8,128)(2,1)S(1)} %add_convert_fusion.1) | copy-start | bytes 393220
  94.6 42.4 %all-to-all-start.1 = ((bf16[64,2,512]{2,1,0:T(2,128)(2,1)}), bf16[64,2,512]{2,1,0:T(2,128)(2,1)S(1)}, u32[]{:S(2)}, u32[]{:S(2)}) async-start(bf16[64,2,512]{2,1,0:T(2,128)(2,1)} %reshape.294), calls=%async_computation.1 | async-start | bytes 262144 | tf_op jit(solution)/shard_map/all_to_all | solution.py:153
  137.0 10.8 %copy-start.6 = (bf16[64,2,512]{2,1,0:T(2,128)(2,1)}, bf16[64,2,512]{2,1,0:T(2,128)(2,1)S(1)}, u32[]{:S(2)}) copy-start(bf16[64,2,512]{2,1,0:T(2,128)(2,1)S(1)} %all-to-all-done.1) | copy-start | bytes 393220
  137.0 37.6 %all-to-all-start = ((bf16[64,2,8192]{2,1,0:T(2,128)(2,1)}), bf16[64,2,8192]{2,1,0:T(2,128)(2,1)}, u32[]{:S(2)}, u32[]{:S(2)}) async-start(bf16[64,2,8192]{2,1,0:T(2,128)(2,1)} %reshape.292), calls=%async_computation | async-start | bytes 4194304 | tf_op jit(solution)/shard_map/all_to_all | solution.py:156
  209.6 3.3 copy-start.8
  215.1 0.7 copy-start.9
  217.2 3.3 copy-start.8
  222.7 0.7 copy-start.9
  224.8 3.3 copy-start.8
  230.3 0.7 copy-start.9
  232.3 3.3 copy-start.8
  237.8 0.7 copy-start.9
  239.9 3.3 copy-start.8
  245.4 0.7 copy-start.9
  247.5 3.3 copy-start.8
  253.0 0.7 copy-start.9
  255.1 3.3 copy-start.8
  260.6 0.7 copy-start.9
  262.7 3.3 copy-start.8
  268.2 0.7 copy-start.9
  353.8 11.3 %copy-start.5 = (bf16[1024,64]{1,0:T(8,128)(2,1)S(1)}, bf16[1024,64]{1,0:T(8,128)(2,1)}, u32[]{:S(2)}) copy-start(bf16[1024,64]{1,0:T(8,128)(2,1)} %get-tuple-element.243) | copy-start | bytes 393220
  356.3 14.9 %all-to-all-start.4 = ((bf16[64,2,512]{2,1,0:T(2,128)(2,1)}), bf16[64,2,512]{2,1,0:T(2,128)(2,1)S(1)}, u32[]{:S(2)}, u32[]{:S(2)}) async-start(bf16[64,2,512]{2,1,0:T(2,128)(2,1)} %reshape.302), calls=%async_computation.5 | async-start | bytes 262144 | tf_op jit(solution)/shard_map/all_to_all | solution.py:199
  371.2 43.6 %all-to-all-start.2 = ((bf16[64,2,512]{2,1,0:T(2,128)(2,1)}), bf16[64,2,512]{2,1,0:T(2,128)(2,1)S(1)}, u32[]{:S(2)}, u32[]{:S(2)}) async-start(bf16[64,2,512]{2,1,0:T(2,128)(2,1)} %reshape.296), calls=%async_computation.2 | async-start | bytes 262144 | tf_op jit(solution)/shard_map/all_to_all | solution.py:170
  414.8 44.7 %all-to-all-start.5 = ((bf16[64,2,8192]{2,1,0:T(2,128)(2,1)}), bf16[64,2,8192]{2,1,0:T(2,128)(2,1)}, u32[]{:S(2)}, u32[]{:S(2)}) async-start(bf16[64,2,8192]{2,1,0:T(2,128)(2,1)} %reshape.300), calls=%async_computation.6 | async-start | bytes 4194304 | tf_op jit(solution)/shard_map/all_to_all | solution.py:206
  424.0 71.3 %reduce-scatter.3.cloned.1.call-start = ((), (), s32[]{:S(2)}) async-start(), calls=%async_computation.8 | async-start | bytes 655360 | tf_op jit(solution)/shard_map/reduce_scatter | solution.py:176
  426.9 117.8 %all-reduce.2.cloned.1.call-start = ((), (), s32[]{:S(2)}) async-start(), calls=%async_computation.9 | async-start | bytes 1048576 | tf_op jit(solution)/shard_map/psum | solution.py:224
  485.5 7.1 copy-start.2
  492.5 2.8 copy-start.4
  492.5 347.0 %reduce-scatter.5.cloned.1.call-start = ((), (), s32[]{:S(2)}) async-start(), calls=%async_computation.10 | async-start | bytes 4259840 | tf_op jit(solution)/shard_map/reduce_scatter | solution.py:180
  495.2 52.0 %copy-start.7 = (bf16[128,512]{1,0:T(8,128)(2,1)S(1)}, bf16[128,512]{1,0:T(8,128)(2,1)}, u32[]{:S(2)}) copy-start(bf16[128,512]{1,0:T(8,128)(2,1)} %param.17) | copy-start | bytes 393220
Sparse Core Ops, SparseCore 0:
  427.3 29.2 reduce-scatter.2
  492.6 52.0 all-reduce.1
  547.8 291.6 reduce-scatter.4
where the time goes:
time: 858 us; the launch traced here: 846 us
  waiting for transfers between devices  393 us (46%)
  local copies, waits for them, and re-layouts  130 us (15%)
  matrix products  115 us (13%)
  other arithmetic  105 us (12%)
  starting transfers between devices  54.6 us (6%)
  blocking collectives  33.2 us (4%)
  between operations  14.5 us (2%)
    reduce_scatter x1, waiting for transfers between devices, body(): lax.psum_scatter(contract(attention, grad_full, 0, 0), 'seq', scatter_dim...  291 us
    dot_general x43, matrix products, contract(): lax.dot_general(left_side, right_side, (((left_axis,), (right_axis,)), ((...  79.5 us
    psum x1, waiting for transfers between devices, body(): lax.psum(grad_normed.astype(jnp.bfloat16), 'tp').astype(jnp.float32)  47.8 us
    unnamed x33, local copies, waits for them, and re-layouts  45.4 us
    all_to_all x1, waiting for transfers between devices, body(): lax.all_to_all(pair_grad.astype(jnp.bfloat16), 'seq', split_axis=0, conca...  31.4 us
    all_to_all x2, other arithmetic, body(): lax.all_to_all(copies(key_value, group_size), 'seq', split_axis=0, concat...  28.3 us
    all_to_all x1, waiting for transfers between devices, body(): lax.all_to_all(copies(key_value, group_size), 'seq', split_axis=0, concat...  20.4 us
    all_gather x1, blocking collectives, body(): lax.all_gather(grad_output, 'tp', axis=1, tiled=True)  18.3 us
  transfers between devices with their start and end apart: 10, of which 5 were waited for; matrix products, arithmetic and copies ran while one was open for 19% of the time, Pallas kernels for 0%

commit v1 on v0

v1 whole, which is shorter than its diff:
```python
import functools

import jax
import jax.numpy as jnp
from jax import lax
from jax.experimental import pallas as pl
from jax.experimental.pallas import tpu as pltpu
from jax.sharding import Mesh, PartitionSpec as P

SPLIT = (2, 4, 4, 2, 4)
AXES = ("zl", "x", "y", "core", "tp")
SEQ = ("zl", "x", "y", "core")
HEADS_OVER = ("zl", "x")

HD = 64
BOOKS = 4
DMAX = 3
VOCAB = 1024
ROWS = 128
WIDTH = 512
LOCAL = 8
TP = 4
MINE = LOCAL * ROWS
TILE = 256
NEGATIVE = -1e30
EPS = 1e-05
F32 = jnp.float32
BF16 = jnp.bfloat16
PARAMS = pltpu.CompilerParams(vmem_limit_bytes=56 * 1024 * 1024)


def mm(left, right, left_axis=1, right_axis=0):
    return lax.dot_general(
        left, right, (((left_axis,), (right_axis,)), ((), ())), preferred_element_type=F32
    )


def ring(distance, count):
    return [(i, (i + distance) % count) for i in range(count)]


def embed_kernel(ids_ref, table_ref, out_ref, total):
    book = pl.program_id(0)
    entries = lax.broadcasted_iota(jnp.int32, (ROWS, VOCAB), 1)
    chosen = jnp.where(entries == ids_ref[0], 1.0, 0.0).astype(BF16)
    looked = mm(chosen, table_ref[0])

    @pl.when(book == 0)
    def _():
        total[...] = looked

    @pl.when(book > 0)
    def _():
        total[...] += looked

    out_ref[...] = total[...].astype(BF16)


def embed(ids, table):
    return pl.pallas_call(
        embed_kernel,
        grid=(BOOKS,),
        in_specs=[
            pl.BlockSpec((1, ROWS, 1), lambda b: (b, 0, 0)),
            pl.BlockSpec((1, VOCAB, WIDTH), lambda b: (b, 0, 0)),
        ],
        out_specs=pl.BlockSpec((ROWS, WIDTH), lambda b: (0, 0)),
        out_shape=jax.ShapeDtypeStruct((ROWS, WIDTH), BF16),
        scratch_shapes=[pltpu.VMEM((ROWS, WIDTH), F32)],
        compiler_params=PARAMS,
        name="embed",
    )(ids, table)


def project_kernel(summed_ref, weight_ref, grad_ref, out_ref, inv_ref, normed, total):
    step = pl.program_id(0)

    @pl.when(step == 0)
    def _():
        squares = jnp.zeros((ROWS, 1), F32)
        for t in range(TP):
            part = summed_ref[t].astype(F32)
            squares += jnp.sum(part * part, axis=1, keepdims=True)
        inv = lax.rsqrt(squares / (TP * WIDTH) + EPS)
        inv_ref[...] = jnp.broadcast_to(inv, (ROWS, 128))
        for t in range(TP):
            normed[t] = (summed_ref[t].astype(F32) * inv).astype(BF16)
        total[...] = jnp.zeros_like(total)

    total[...] += mm(normed[step], weight_ref[...])

    @pl.when(step == TP - 1)
    def _():
        done = total[...].astype(BF16)
        grads = grad_ref[...]
        for h in range(LOCAL):
            q, k, v = (done[:, j * WIDTH + h * HD : j * WIDTH + (h + 1) * HD] for j in range(3))
            out_ref[h] = jnp.concatenate([k, v, q, grads[:, h * HD : (h + 1) * HD]], axis=1)


def project(summed_all, weight, grads):
    return pl.pallas_call(
        project_kernel,
        grid=(TP,),
        in_specs=[
            pl.BlockSpec((TP, ROWS, WIDTH), lambda s: (0, 0, 0)),
            pl.BlockSpec((WIDTH, 3 * WIDTH), lambda s: (s, 0)),
            pl.BlockSpec((ROWS, WIDTH), lambda s: (0, 0)),
        ],
        out_specs=[
            pl.BlockSpec((LOCAL, ROWS, 4 * HD), lambda s: (0, 0, 0)),
            pl.BlockSpec((ROWS, 128), lambda s: (0, 0)),
        ],
        out_shape=[
            jax.ShapeDtypeStruct((LOCAL, ROWS, 4 * HD), BF16),
            jax.ShapeDtypeStruct((ROWS, 128), F32),
        ],
        scratch_shapes=[
            pltpu.VMEM((TP, ROWS, WIDTH), BF16),
            pltpu.VMEM((ROWS, 3 * WIDTH), F32),
        ],
        compiler_params=PARAMS,
        name="project",
    )(summed_all, weight, grads)


def flip(block):
    return jnp.transpose(block.astype(F32))


def frame_gap():
    keys = lax.broadcasted_iota(jnp.int32, (TILE, TILE), 0)
    queries = lax.broadcasted_iota(jnp.int32, (TILE, TILE), 1)
    frame = lambda i: lax.shift_right_logical(i, 7) * (LOCAL * ROWS) + lax.bitwise_and(i, ROWS - 1)
    return frame(keys) - frame(queries)


def chunk_limit(place_ref, back, other):
    y, core = place_ref[0], place_ref[1]
    chunk = lax.bitwise_and(y - back, 3) * 2 + (1 - core if other else core)
    return (2 * y + core - chunk) * ROWS


def masked(scores, gap, limit):
    last = jnp.where(gap <= limit, scores[scores.shape[0] - TILE :], NEGATIVE)
    if scores.shape[0] == TILE:
        return last
    return jnp.concatenate([scores[: scores.shape[0] - TILE], last], axis=0)


def pack(rows):
    halves = rows.reshape(LOCAL, 2, HD, HD)
    return jnp.concatenate([halves[:, 0], halves[:, 1]], axis=2)


def forward_kernel(place_ref, mine_ref, same_ref, other_ref, out_ref, stat_ref, queries, total, top):
    mine = flip(mine_ref[:, 2 * HD :])
    feature = lax.broadcasted_iota(jnp.int32, (2 * HD, MINE), 0)
    queries[...] = jnp.where(feature < HD, mine * (HD**-0.5), 0.0).astype(BF16)
    total[...] = jnp.zeros_like(total)
    top[...] = jnp.full_like(top, NEGATIVE)
    gap = frame_gap()

    def visit(back, carried):
        for other, ref in enumerate((same_ref, other_ref)):
            limit = chunk_limit(place_ref, back, other)
            pair = ref[back]
            values = jnp.where(feature < HD, 1.0, flip(pair)).astype(BF16)
            for a in range(MINE // TILE):
                count, at = TILE * (a + 1), slice(TILE * a, TILE * (a + 1))
                scores = masked(mm(pair[:count], queries[:, at]), gap, limit)
                old = top[:, at]
                new = jnp.maximum(old, jnp.max(scores, axis=0, keepdims=True))
                weights = jnp.exp(scores - new).astype(BF16)
                total[:, at] = total[:, at] * jnp.exp(old - new) + mm(values[:, :count], weights)
                top[:, at] = new
        return carried

    lax.fori_loop(0, 4, visit, 0)
    row_total = total[0:1]
    attended = (total[HD:] / row_total).astype(BF16)
    stat_ref[0:1] = top[...] + jnp.log(row_total)
    stat_ref[1:2] = jnp.sum(mine[HD:] * attended.astype(F32), axis=0, keepdims=True)
    out_ref[...] = pack(jnp.transpose(attended.astype(F32))).astype(BF16)


def full(*shape):
    return pl.BlockSpec(shape, lambda *_: (0,) * len(shape))


SMEM = pl.BlockSpec(memory_space=pltpu.SMEM)


def attend(place, mine, same, other):
    return pl.pallas_call(
        forward_kernel,
        in_specs=[
            SMEM,
            full(MINE, 4 * HD),
            full(4, MINE, 2 * HD),
            full(4, MINE, 2 * HD),
        ],
        out_specs=[full(LOCAL, HD, 2 * HD), full(8, MINE)],
        out_shape=[
            jax.ShapeDtypeStruct((LOCAL, HD, 2 * HD), BF16),
            jax.ShapeDtypeStruct((8, MINE), F32),
        ],
        scratch_shapes=[
            pltpu.VMEM((2 * HD, MINE), BF16),
            pltpu.VMEM((2 * HD, MINE), F32),
            pltpu.VMEM((1, MINE), F32),
        ],
        compiler_params=PARAMS,
        name="attend",
    )(place, mine, same, other)


def backward_kernel(
    place_ref, mine_ref, stat_ref, same_ref, other_ref,
    to_same_ref, to_other_ref, out_ref,
    columns, rows, query_total, pair_total,
):
    mine = mine_ref[:, 2 * HD :]
    first = lax.broadcasted_iota(jnp.int32, (MINE, 2 * HD), 1) < HD
    rows[0] = jnp.where(first, mine.astype(F32) * (HD**-0.5), 0.0).astype(BF16)
    rows[1] = jnp.where(first, 0.0, mine.astype(F32)).astype(BF16)
    columns[0] = flip(rows[0]).astype(BF16)
    columns[1] = flip(rows[1]).astype(BF16)
    query_total[...] = jnp.zeros_like(query_total)
    gap = frame_gap()

    def visit(back, carried):
        for other, (ref, to_ref) in enumerate(((same_ref, to_same_ref), (other_ref, to_other_ref))):
            limit = chunk_limit(place_ref, back, other)
            pair = ref[back]
            turned = flip(pair).astype(BF16)
            for a in reversed(range(MINE // TILE)):
                count, at = TILE * (a + 1), slice(TILE * a, TILE * (a + 1))
                scores = masked(mm(pair[:count], columns[0, :, at]), gap, limit)
                chances = jnp.exp(scores - stat_ref[0:1, at])
                grads = mm(pair[:count], columns[1, :, at])
                score_grad = (chances * (grads - stat_ref[1:2, at])).astype(BF16)
                query_total[:, at] += mm(turned[:, :count], score_grad)
                added = mm(score_grad, rows[0, at]) + mm(chances.astype(BF16), rows[1, at])
                if count == MINE:
                    pair_total[...] = added
                else:
                    pair_total[:count] += added
            to_ref[back] = pair_total[...].astype(BF16)
        return carried

    lax.fori_loop(0, 4, visit, 0)
    out_ref[...] = pack(jnp.transpose(query_total[:HD] * (HD**-0.5))).astype(BF16)


def attend_back(place, mine, stat, same, other):
    return pl.pallas_call(
        backward_kernel,
        in_specs=[
            SMEM,
            full(MINE, 4 * HD),
            full(8, MINE),
            full(4, MINE, 2 * HD),
            full(4, MINE, 2 * HD),
        ],
        out_specs=[full(4, MINE, 2 * HD), full(4, MINE, 2 * HD), full(LOCAL, HD, 2 * HD)],
        out_shape=[
            jax.ShapeDtypeStruct((4, MINE, 2 * HD), BF16),
            jax.ShapeDtypeStruct((4, MINE, 2 * HD), BF16),
            jax.ShapeDtypeStruct((LOCAL, HD, 2 * HD), BF16),
        ],
        scratch_shapes=[
            pltpu.VMEM((2, 2 * HD, MINE), BF16),
            pltpu.VMEM((2, MINE, 2 * HD), BF16),
            pltpu.VMEM((2 * HD, MINE), F32),
            pltpu.VMEM((MINE, 2 * HD), F32),
        ],
        compiler_params=PARAMS,
        name="attend_back",
    )(place, mine, stat, same, other)


def unpack(packed):
    return jnp.concatenate([packed[:, :HD], packed[:, HD:]], axis=0)


def output_kernel(heads_ref, grad_ref, weight_ref, share_ref, weight_grad_ref):
    attention = jnp.concatenate([unpack(heads_ref[h]) for h in range(LOCAL)], axis=1)
    for t in range(TP):
        at = slice(t * WIDTH, (t + 1) * WIDTH)
        share_ref[t] = mm(attention, weight_ref[:, at]).astype(BF16)
        weight_grad_ref[at] = mm(grad_ref[t], attention, 0, 0).astype(BF16)


def output_side(heads, grad_all, weight):
    return pl.pallas_call(
        output_kernel,
        in_specs=[full(LOCAL, HD, 2 * HD), full(TP, ROWS, WIDTH), full(WIDTH, TP * WIDTH)],
        out_specs=[full(TP, ROWS, WIDTH), full(TP * WIDTH, WIDTH)],
        out_shape=[
            jax.ShapeDtypeStruct((TP, ROWS, WIDTH), BF16),
            jax.ShapeDtypeStruct((TP * WIDTH, WIDTH), BF16),
        ],
        compiler_params=PARAMS,
        name="output_side",
    )(heads, grad_all, weight)


def weight_sum_kernel(parts_ref, out_ref):
    total = parts_ref[0].astype(F32)
    for i in range(1, parts_ref.shape[0]):
        total += parts_ref[i].astype(F32)
    out_ref[...] = jnp.transpose(total)


def weight_sum(parts):
    return pl.pallas_call(
        weight_sum_kernel,
        in_specs=[full(*parts.shape)],
        out_specs=full(WIDTH, parts.shape[1]),
        out_shape=jax.ShapeDtypeStruct((WIDTH, parts.shape[1]), F32),
        compiler_params=PARAMS,
        name="weight_sum",
    )(parts)


EXTRA = 16


def input_kernel(back_ref, weight_ref, summed_ref, inv_ref, out_ref, triple, centre):
    step = pl.program_id(0)

    @pl.when(step == 0)
    def _():
        pairs = [back_ref[h, :ROWS] for h in range(LOCAL)]
        parts = [unpack(back_ref[h, ROWS:]) for h in range(LOCAL)]
        parts += [pair[:, :HD] for pair in pairs] + [pair[:, HD:] for pair in pairs]
        triple[...] = jnp.concatenate(parts, axis=1)
        centre[...] = jnp.zeros_like(centre)

    part = mm(triple[...], weight_ref[...], 1, 1)
    normed = summed_ref[step].astype(F32) * inv_ref[:, 0:1]
    centre[...] += jnp.sum(part * normed, axis=1, keepdims=True)
    out_ref[step, :ROWS] = part.astype(BF16)

    @pl.when(step == TP - 1)
    def _():
        line = jnp.transpose(centre[...])[0:1]
        high = line.astype(BF16).astype(F32)
        middle = (line - high).astype(BF16).astype(F32)
        low = line - high - middle
        zero = jnp.zeros((1, ROWS), F32)
        block = jnp.concatenate([high, middle, low] + [zero] * (EXTRA - 3), axis=0)
        block = jnp.concatenate([block, jnp.zeros((EXTRA, WIDTH - ROWS), F32)], axis=1)
        for t in range(TP):
            out_ref[t, ROWS:] = block.astype(BF16)


def input_side(back, weight, summed_all, inv):
    return pl.pallas_call(
        input_kernel,
        grid=(TP,),
        in_specs=[
            full(LOCAL, ROWS + HD, 2 * HD),
            pl.BlockSpec((WIDTH, 3 * WIDTH), lambda s: (s, 0)),
            full(TP, ROWS, WIDTH),
            full(ROWS, 128),
        ],
        out_specs=full(TP, ROWS + EXTRA, WIDTH),
        out_shape=jax.ShapeDtypeStruct((TP, ROWS + EXTRA, WIDTH), BF16),
        scratch_shapes=[pltpu.VMEM((ROWS, 3 * WIDTH), BF16), pltpu.VMEM((ROWS, 128), F32)],
        compiler_params=PARAMS,
        name="input_side",
    )(back, weight, summed_all, inv)


def finish_kernel(parts_ref, summed_ref, inv_ref, grad_ref, out_ref):
    total = sum(parts_ref[t, :ROWS].astype(F32) for t in range(TP))
    lines = sum(parts_ref[t, ROWS:, :ROWS].astype(F32) for t in range(TP))
    line = jnp.sum(lines, axis=0, keepdims=True) / (TP * WIDTH)
    centre = jnp.transpose(jnp.broadcast_to(line, (ROWS, ROWS)))[:, 0:1]
    inv = inv_ref[:, 0:1]
    normed = summed_ref[...].astype(F32) * inv
    out_ref[...] = grad_ref[...].astype(F32) + inv * (total - normed * centre)


def finish(parts, summed, inv, grad):
    return pl.pallas_call(
        finish_kernel,
        in_specs=[
            full(TP, ROWS + EXTRA, WIDTH),
            full(ROWS, WIDTH),
            full(ROWS, 128),
            full(ROWS, WIDTH),
        ],
        out_specs=full(ROWS, WIDTH),
        out_shape=jax.ShapeDtypeStruct((ROWS, WIDTH), F32),
        compiler_params=PARAMS,
        name="finish",
    )(parts, summed, inv, grad)


def pick_ids(code_ids, delays):
    seq_index = lax.axis_index(SEQ)
    count = lax.axis_size(SEQ)
    route = [(i, i + 1) for i in range(count - 1)]
    before = lax.ppermute(code_ids[:, ROWS - DMAX :], SEQ, route)
    joined = jnp.concatenate([before, code_ids], axis=1)
    picked = joined[:, DMAX:]
    for delay in range(1, DMAX + 1):
        moved = joined[:, DMAX - delay : DMAX - delay + ROWS]
        picked = jnp.where(delays[:, None] == delay, moved, picked)
    frames = seq_index * ROWS + jnp.arange(ROWS, dtype=jnp.int32)
    return jnp.where(frames[None, :] >= delays[:, None], picked, -1)[:, :, None]


def body(code_ids, delays, embed_table, project_in, project_out, grad_output):
    place = jnp.stack([lax.axis_index("y"), lax.axis_index("core")]).astype(jnp.int32)
    weight_in = project_in.reshape(TP * WIDTH, 3 * WIDTH)
    grad_all = lax.all_gather(grad_output, "tp", axis=0)
    summed = embed(pick_ids(code_ids, delays), embed_table)
    summed_all = lax.all_gather(summed, "tp", axis=0)
    grad_attention = sum(
        mm(grad_all[t], project_out[:, t * WIDTH : (t + 1) * WIDTH], 1, 1) for t in range(TP)
    ).astype(BF16)
    blocks, inv = project(summed_all, weight_in, grad_attention)
    mine = lax.all_to_all(blocks, HEADS_OVER, 0, 0, tiled=True).reshape(MINE, 4 * HD)

    own = mine[:, : 2 * HD]
    same = jnp.stack([own] + [lax.ppermute(own, "y", ring(k, 4)) for k in range(1, 4)])
    other = lax.ppermute(same, "core", [(0, 1), (1, 0)])
    attended, stat = attend(place, mine, same, other)

    heads = lax.all_to_all(attended, HEADS_OVER, 0, 0, tiled=True)
    shares, weight_grads = output_side(heads, grad_all, project_out)
    shares = lax.all_to_all(shares, "tp", 0, 0, tiled=True)
    layer_output = (
        summed.astype(F32) + sum(shares[t].astype(F32) for t in range(TP))
    ).astype(BF16)
    weight_parts = lax.all_to_all(
        weight_grads.reshape(64, TP * WIDTH // 64, WIDTH), SEQ, 0, 0, tiled=True
    )
    grad_project_out = weight_sum(weight_parts)

    to_same, to_other, query_grads = attend_back(place, mine, stat, same, other)
    from_other = lax.ppermute(to_other, "core", [(0, 1), (1, 0)])
    both = (to_same.astype(F32) + from_other.astype(F32)).astype(BF16)
    pair_grads = both[0].astype(F32)
    for k in range(1, 4):
        pair_grads += lax.ppermute(both[k], "y", ring(-k, 4)).astype(F32)
    packed = jnp.concatenate(
        [pair_grads.astype(BF16).reshape(LOCAL, ROWS, 2 * HD), query_grads], axis=1
    )
    back = lax.all_to_all(packed, HEADS_OVER, 0, 0, tiled=True)
    parts = input_side(back, weight_in, summed_all, inv)
    parts = lax.all_to_all(parts, "tp", 0, 0, tiled=True)
    grad_embed = finish(parts, summed, inv, grad_output)
    return layer_output, grad_embed, grad_project_out


def solution(mesh):
    fine = Mesh(mesh.devices.reshape(SPLIT), AXES)
    return jax.shard_map(
        body,
        mesh=fine,
        in_specs=(
            P(None, SEQ),
            P(),
            P(None, None, "tp"),
            P(None, None, "tp"),
            P("tp", None),
            P(SEQ, "tp"),
        ),
        out_specs=(P(SEQ, "tp"), P(SEQ, "tp"), P("tp", SEQ)),
        check_vma=False,
    )
```

time: 858 us -> 254 us (0.30)
  waiting for transfers between devices: 393 us -> 55.3 us
  matrix products: 115 us -> 4.17 us
  local copies, waits for them, and re-layouts: 130 us -> 23.5 us
  other arithmetic: 105 us -> 4.65 us
  Pallas kernels: 0 us -> 59.7 us
  blocking collectives: 33.2 us -> 67.2 us
  starting transfers between devices: 54.6 us -> 34.5 us
  between operations: 14.5 us -> 0.8 us
    reduce_scatter x2 -> x0, waiting for transfers between devices: 291 us -> none  [the longest x1 291 us: body(): lax.psum_scatter(contract(attention, grad_full, 0, 0), 'seq', scatter_dim...]
    dot_general x61 -> x4, matrix products: 115 us -> 4.17 us  [mm(): lax.dot_general(left, right, (((left_axis,), (right_axis,)), ((), ())), p...]
    pallas_call x0 -> x8, Pallas kernels: none -> 59.7 us  [the longest x1 18.1 us: attend_back(): pl.pallas_call(backward_kernel, in_specs=[SMEM, full(MINE, 4 * HD), full(...]
    psum x1 -> x0, waiting for transfers between devices: 47.8 us -> none  [body(): lax.psum(grad_normed.astype(jnp.bfloat16), 'tp').astype(jnp.float32)]
    all_to_all x9 -> x0, other arithmetic: 36.7 us -> none  [the longest x2 28.3 us: body(): lax.all_to_all(copies(key_value, group_size), 'seq', split_axis=0, concat...]
    all_to_all x0 -> x2, blocking collectives: none -> 33.3 us  [the longest x1 16.8 us: body(): lax.all_to_all(blocks, HEADS_OVER, 0, 0, tiled=True).reshape(MINE, 4 * HD)]
    unnamed x33 -> x26, local copies, waits for them, and re-layouts: 45.4 us -> 13 us
    all_to_all x6 -> x4, starting transfers between devices: 52.5 us -> 22.3 us  [the longest x1 9.17 us: body(): lax.all_to_all(weight_grads.reshape(64, TP * WIDTH // 64, WIDTH), SEQ, 0,...]
  transfers between devices with their start and end apart: 10 -> 13, of which waited for: 5 -> 10; matrix products, arithmetic and copies ran while one was open for 19% -> 10% of each run, Pallas kernels for 0% -> 5%
where the time goes in v1:
time: 254 us; the launch traced here: 250 us
  blocking collectives  67.2 us (26%)
  Pallas kernels  59.7 us (24%)
  waiting for transfers between devices  55.3 us (22%)
  starting transfers between devices  34.5 us (14%)
  local copies, waits for them, and re-layouts  23.5 us (9%)
  other arithmetic  4.65 us (2%)
  matrix products  4.17 us (2%)
    all_to_all x1, waiting for transfers between devices, body(): lax.all_to_all(weight_grads.reshape(64, TP * WIDTH // 64, WIDTH), SEQ, 0,...  25.7 us
    all_gather x1, blocking collectives, body(): grad_all = lax.all_gather(grad_output, 'tp', axis=0)  18.3 us
    pallas_call x1, Pallas kernels, attend_back(): pl.pallas_call(backward_kernel, in_specs=[SMEM, full(MINE, 4 * HD), full(...  18.1 us
    all_to_all x1, blocking collectives, body(): lax.all_to_all(blocks, HEADS_OVER, 0, 0, tiled=True).reshape(MINE, 4 * HD)  16.8 us
    all_to_all x1, blocking collectives, body(): parts = lax.all_to_all(parts, 'tp', 0, 0, tiled=True)  16.4 us
    pallas_call x1, Pallas kernels, attend(): pl.pallas_call(forward_kernel, in_specs=[SMEM, full(MINE, 4 * HD), full(4...  16 us
    all_gather x1, blocking collectives, body(): summed_all = lax.all_gather(summed, 'tp', axis=0)  15.7 us
    unnamed x26, local copies, waits for them, and re-layouts  13 us
  transfers between devices with their start and end apart: 13, of which 10 were waited for; matrix products, arithmetic and copies ran while one was open for 10% of the time, Pallas kernels for 5%

profile of v1, /device:TPU:64, one launch (start us, length us, event | category | flops | bytes accessed | tf_op | source)
XLA Modules:
  0.0 249.8 jit_solution(15465469189170529451)
XLA Ops:
  0.6 0.9 slice.63
  1.5 1.7 collective-permute-start
  3.3 0.7 broadcast_compare_fusion.2
  4.0 18.3 %all-gather.1 = bf16[512,512]{1,0:T(8,128)(2,1)S(1)} all-gather(bf16[128,512]{1,0:T(8,128)(2,1)} %grad_ref.1), channel_id=3, replica_groups=mesh['zl'=2,'x'=4,'y'=4,'core'=2,'tp'=4] {'tp'}, dimensions={0}, use_global_device_ids=true | all-gather | bytes 655360 | tf_op jit(solution)/shard_map/all_gather | solution.py:420
  22.2 1.5 fusion.7
  23.8 1.4 convolution_add_fusion.2
  25.5 1.0 fusion.grad_ref
  26.4 8.8 %copy.12 = bf16[2048,3,512]{0,2,1:T(8,128)(2,1)} copy(bf16[2048,3,512]{2,0,1:T(8,128)(2,1)} %param.9) | data formatting | bytes 12582912 | tf_op args[3]
  35.3 8.7 %copy.13.weight_ref = bf16[2048,1536]{1,0:T(8,128)(2,1)} copy(bf16[2048,1536]{0,1:T(8,128)(2,1)} %bitcast.30) | data formatting | bytes 12582912 | tf_op jit(solution)/shard_map/reshape | solution.py:419
  44.0 0.9 copy.11.ids_ref
  44.9 4.5 %embed.1.summed_ref = bf16[128,512]{1,0:T(8,128)(2,1)} custom-call(s32[4,128,1]{2,1,0:T(8,128)} %copy.11.ids_ref, bf16[4,1024,512]{2,1,0:T(8,128)(2,1)} %table_ref.1), custom_call_target="tpu_custom_call" | custom-call | tf_op jit(solution)/shard_map/embed/pallas_call | solution.py:60
  49.3 15.7 %all-gather = bf16[512,512]{1,0:T(8,128)(2,1)} all-gather(bf16[128,512]{1,0:T(8,128)(2,1)} %embed.1.summed_ref), channel_id=2, replica_groups=mesh['zl'=2,'x'=4,'y'=4,'core'=2,'tp'=4] {'tp'}, dimensions={0}, use_global_device_ids=true | all-gather | bytes 655360 | tf_op jit(solution)/shard_map/all_gather | solution.py:422
  65.0 5.6 %project.1 = (bf16[8,128,256]{2,1,0:T(8,128)(2,1)}, f32[128,128]{1,0:T(8,128)}) custom-call(bf16[4,128,512]{2,1,0:T(8,128)(2,1)} %bitcast.35, bf16[2048,1536]{1,0:T(8,128)(2,1)} %copy.13.weight_ref, bf16[128,512]{1,0:T(8,128)(2,1)} %fusion.grad_ref), custom_call_target="tpu_custom_call" | custom-call | tf_op jit(solution)/shard_map/project/pallas_call | solution.py:102
  70.6 16.8 %all_to_all.30 = bf16[8,128,256]{2,1,0:T(8,128)(2,1)S(1)} all-to-all(bf16[8,128,256]{2,1,0:T(8,128)(2,1)} %get-tuple-element.12), channel_id=1, replica_groups=mesh['zl'=2,'x'=4,'y'=4,'core'=2,'tp'=4] {'zl','x'}, dimensions={0} | all-to-all | bytes 1048576 | tf_op jit(solution)/shard_map/all_to_all | solution.py:427
  87.5 2.5 collective-permute-start.2
  89.9 1.0 collective-permute-start.1
  91.0 2.2 collective-permute-start.3
  93.2 4.4 %collective-permute-done.2 = bf16[1024,128]{1,0:T(8,128)(2,1)S(1)} collective-permute-done((bf16[1024,128]{1,0:T(8,128)(2,1)S(1)}, bf16[1024,128]{1,0:T(8,128)(2,1)S(1)}, u32[]{:S(2)}, u32[]{:S(2)}) %collective-permute-start.2) | collective-permute-done | bytes 262176 | tf_op jit(solution)/shard_map/ppermute | solution.py:430
  97.6 2.7 %collective-permute-done.1 = bf16[1024,128]{1,0:T(8,128)(2,1)S(1)} collective-permute-done((bf16[1024,128]{1,0:T(8,128)(2,1)S(1)}, bf16[1024,128]{1,0:T(8,128)(2,1)S(1)}, u32[]{:S(2)}, u32[]{:S(2)}) %collective-permute-start.1) | collective-permute-done | bytes 262176 | tf_op jit(solution)/shard_map/ppermute | solution.py:430
  100.7 0.6 pad_add_fusion.1.place_ref
  101.3 2.1 collective-permute-done.4.other_ref
  103.4 1.1 copy-done.5
  104.4 16.0 %attend.1 = (bf16[8,64,128]{2,1,0:T(8,128)(2,1)}, f32[8,1024]{1,0:T(8,128)}) custom-call(s32[2]{0:T(128)} %pad_add_fusion.1.place_ref, bf16[1024,256]{1,0:T(8,128)(2,1)} %bitcast.32, bf16[4,1024,128]{2,1,0:T(8,128)(2,1)} %copy-done, bf16[4,1024,128]{2,1,0:T(8,128)(2,1)} %copy-done.5), custom_call_target="tpu_custom_call" | custom-call | tf_op jit(solution)/shard_map/attend/pallas_call | solution.py:195
  120.4 18.1 %attend_back.1 = (bf16[4,1024,128]{2,1,0:T(8,128)(2,1)}, bf16[4,1024,128]{2,1,0:T(8,128)(2,1)}, bf16[8,64,128]{2,1,0:T(8,128)(2,1)}) custom-call(s32[2]{0:T(128)} %pad_add_fusion.1.place_ref, bf16[1024,256]{1,0:T(8,128)(2,1)} %bitcast.33, f32[8,1024]{1,0:T(8,128)} %get-tuple-element.15.stat_ref, bf16[4,1024,128]{2,1,0:T(8,128)(2,1)} %copy-done, ...), custom_call_target="tpu_custom_call" | custom-call | tf_op jit(solution)/shard_map/attend_back/pallas_call | solution.py:257
  138.7 2.7 %collective-permute-done.5 = bf16[4,1024,128]{2,1,0:T(8,128)(2,1)S(1)} collective-permute-done((bf16[4,1024,128]{2,1,0:T(8,128)(2,1)}, bf16[4,1024,128]{2,1,0:T(8,128)(2,1)S(1)}, u32[]{:S(2)}, u32[]{:S(2)}) %collective-permute-start.5) | collective-permute-done | bytes 1048608 | tf_op jit(solution)/shard_map/ppermute | solution.py:446
  141.4 1.5 add_convert_fusion
  143.0 1.0 collective-permute-start.6
  144.0 1.1 collective-permute-start.8
  145.1 2.2 collective-permute-start.7
  147.3 4.0 %all-to-all-start.1 = ((bf16[8,64,128]{2,1,0:T(8,128)(2,1)}), bf16[8,64,128]{2,1,0:T(8,128)(2,1)S(1)}, u32[]{:S(2)}, u32[]{:S(2)}) async-start(bf16[8,64,128]{2,1,0:T(8,128)(2,1)} %get-tuple-element.13), calls=%async_computation.1 | async-start | bytes 262144 | tf_op jit(solution)/shard_map/all_to_all | solution.py:434
  151.3 0.9 collective-permute-done.6
  152.2 2.2 collective-permute-done.8
  154.4 4.5 %collective-permute-done.7 = bf16[1024,128]{1,0:T(8,128)(2,1)S(1)} collective-permute-done((bf16[1024,128]{1,0:T(8,128)(2,1)S(1)}, bf16[1024,128]{1,0:T(8,128)(2,1)S(1)}, u32[]{:S(2)}, u32[]{:S(2)}) %collective-permute-start.7) | collective-permute-done | bytes 262176 | tf_op jit(solution)/shard_map/ppermute | solution.py:450
  159.1 0.8 pad_maximum_fusion.1
  159.9 4.0 %all-to-all-start.3 = ((bf16[8,192,128]{2,1,0:T(8,128)(2,1)}), bf16[8,192,128]{2,1,0:T(8,128)(2,1)S(1)}, u32[]{:S(2)}, u32[]{:S(2)}) async-start(bf16[8,192,128]{2,1,0:T(8,128)(2,1)} %pad_maximum_fusion.1), calls=%async_computation.3 | async-start | bytes 786432 | tf_op jit(solution)/shard_map/all_to_all | solution.py:454
  163.9 4.3 %output_side.1 = (bf16[4,128,512]{2,1,0:T(8,128)(2,1)}, bf16[2048,512]{1,0:T(8,128)(2,1)}) custom-call(bf16[8,64,128]{2,1,0:T(8,128)(2,1)} %copy-done.8, bf16[4,128,512]{2,1,0:T(8,128)(2,1)} %bitcast.34, bf16[512,2048]{1,0:T(8,128)(2,1)} %weight_ref.1), custom_call_target="tpu_custom_call" | custom-call | tf_op jit(solution)/shard_map/output_side/pallas_call | solution.py:296
  168.3 3.4 %all-to-all-done.3.back_ref = bf16[8,192,128]{2,1,0:T(8,128)(2,1)S(1)} async-done(((bf16[8,192,128]{2,1,0:T(8,128)(2,1)}), bf16[8,192,128]{2,1,0:T(8,128)(2,1)S(1)}, u32[]{:S(2)}, u32[]{:S(2)}) %all-to-all-start.3) | async-done | bytes 393248 | tf_op jit(solution)/shard_map/all_to_all | solution.py:454
  171.7 5.1 %all-to-all-start.2 = ((bf16[4,128,512]{2,1,0:T(8,128)(2,1)}), bf16[4,128,512]{2,1,0:T(8,128)(2,1)S(1)}, u32[]{:S(2)}, u32[]{:S(2)}) async-start(bf16[4,128,512]{2,1,0:T(8,128)(2,1)} %get-tuple-element.14), calls=%async_computation.2 | async-start | bytes 1048576 | tf_op jit(solution)/shard_map/all_to_all | solution.py:436
  176.8 6.5 %input_side.1 = bf16[4,144,512]{2,1,0:T(8,128)(2,1)} custom-call(bf16[8,192,128]{2,1,0:T(8,128)(2,1)} %copy-done.7, bf16[2048,1536]{1,0:T(8,128)(2,1)} %copy.13.weight_ref, bf16[4,128,512]{2,1,0:T(8,128)(2,1)} %bitcast.36, f32[128,128]{1,0:T(8,128)} %get-tuple-element.19.inv_ref), custom_call_target="tpu_custom_call" | custom-call | tf_op jit(solution)/shard_map/input_side/pallas_call | solution.py:360
  183.3 6.6 %all-to-all-done.2 = bf16[4,128,512]{2,1,0:T(8,128)(2,1)S(1)} async-done(((bf16[4,128,512]{2,1,0:T(8,128)(2,1)}), bf16[4,128,512]{2,1,0:T(8,128)(2,1)S(1)}, u32[]{:S(2)}, u32[]{:S(2)}) %all-to-all-start.2) | async-done | bytes 524320 | tf_op jit(solution)/shard_map/all_to_all | solution.py:436
  189.9 16.4 %all_to_all.31.parts_ref = bf16[4,144,512]{2,1,0:T(8,128)(2,1)} all-to-all(bf16[4,144,512]{2,1,0:T(8,128)(2,1)} %input_side.1), channel_id=1, replica_groups=mesh['zl'=2,'x'=4,'y'=4,'core'=2,'tp'=4] {'tp'}, dimensions={0} | all-to-all | bytes 1179648 | tf_op jit(solution)/shard_map/all_to_all | solution.py:456
  206.4 9.2 %all-to-all-start.5 = ((bf16[64,32,512]{2,1,0:T(8,128)(2,1)}), bf16[64,32,512]{2,1,0:T(8,128)(2,1)S(1)}, u32[]{:S(2)}, u32[]{:S(2)}) async-start(bf16[64,32,512]{2,1,0:T(8,128)(2,1)} %bitcast.37), calls=%async_computation.5 | async-start | bytes 4194304 | tf_op jit(solution)/shard_map/all_to_all | solution.py:440
  215.6 0.7 fusion.9
  216.3 2.1 finish.1
  218.4 25.7 %all-to-all-done.5.parts_ref = bf16[64,32,512]{2,1,0:T(8,128)(2,1)S(1)} async-done(((bf16[64,32,512]{2,1,0:T(8,128)(2,1)}), bf16[64,32,512]{2,1,0:T(8,128)(2,1)S(1)}, u32[]{:S(2)}, u32[]{:S(2)}) %all-to-all-start.5) | async-done | bytes 2097184 | tf_op jit(solution)/shard_map/all_to_all | solution.py:440
  244.0 1.3 copy-done.2
  245.4 2.7 %weight_sum.1 = f32[512,32]{1,0:T(8,128)} custom-call(bf16[64,32,512]{2,1,0:T(8,128)(2,1)} %copy-done.2), custom_call_target="tpu_custom_call" | custom-call | tf_op jit(solution)/shard_map/weight_sum/pallas_call | solution.py:317
  248.1 1.7 copy.15
  (34 shorter events, 1.2 us)
Async XLA Ops:
  0.6 24.5 %copy-start.1 = (bf16[512,2048]{1,0:T(8,128)(2,1)S(1)}, bf16[512,2048]{1,0:T(8,128)(2,1)}, u32[]{:S(2)}) copy-start(bf16[512,2048]{1,0:T(8,128)(2,1)} %weight_ref.1) | copy-start | bytes 6291460
  1.5 42.4 %collective-permute-start = (s32[4,3]{1,0:T(4,128)S(1)}, s32[4,3]{1,0:T(4,128)S(1)}, u32[]{:S(2)}, u32[]{:S(2)}) collective-permute-start(s32[4,3]{1,0:T(4,128)S(1)} %slice.63), channel_id=1, source_target_pairs={{0,4},{4,8},{8,12},{12,16},{16,20},{20,24},{24,28},{28,32},{32,36}... | collective-permute-start | bytes 152 | tf_op jit(solution)/shard_map/ppermute | solution.py:407
  22.2 4.2 %copy-start.4 = (bf16[512,512]{1,0:T(8,128)(2,1)}, bf16[512,512]{1,0:T(8,128)(2,1)S(1)}, u32[]{:S(2)}) copy-start(bf16[512,512]{1,0:T(8,128)(2,1)S(1)} %all-gather.1) | copy-start | bytes 1572868
  35.3 8.7 %copy-start.10 = (s32[4,128]{1,0:T(4,128)S(1)}, s32[4,128]{1,0:T(4,128)}, u32[]{:S(2)}) copy-start(s32[4,128]{1,0:T(4,128)} %param.6) | copy-start | bytes 6148
  35.3 8.7 %copy-start.11 = (s32[4]{0:T(128)S(1)}, s32[4]{0:T(128)}, u32[]{:S(2)}) copy-start(s32[4]{0:T(128)} %param.7) | copy-start | bytes 52
  87.4 15.9 %copy-start.3 = (bf16[8,128,256]{2,1,0:T(8,128)(2,1)}, bf16[8,128,256]{2,1,0:T(8,128)(2,1)S(1)}, u32[]{:S(2)}) copy-start(bf16[8,128,256]{2,1,0:T(8,128)(2,1)S(1)} %all_to_all.30) | copy-start | bytes 1572868
  87.5 10.1 %collective-permute-start.2 = (bf16[1024,128]{1,0:T(8,128)(2,1)S(1)}, bf16[1024,128]{1,0:T(8,128)(2,1)S(1)}, u32[]{:S(2)}, u32[]{:S(2)}) collective-permute-start(bf16[1024,128]{1,0:T(8,128)(2,1)S(1)} %get-tuple-element.31), channel_id=1, source_target_pairs={{0,16},{8,24},{16,0},{24,8},{1,17},{9,25},{17,1},{25,9},{2,18},{10... | collective-permute-start | bytes 786440 | tf_op jit(solution)/shard_map/ppermute | solution.py:430
  89.9 10.3 %collective-permute-start.1 = (bf16[1024,128]{1,0:T(8,128)(2,1)S(1)}, bf16[1024,128]{1,0:T(8,128)(2,1)S(1)}, u32[]{:S(2)}, u32[]{:S(2)}) collective-permute-start(bf16[1024,128]{1,0:T(8,128)(2,1)S(1)} %get-tuple-element.31), channel_id=1, source_target_pairs={{0,8},{8,16},{16,24},{24,0},{1,9},{9,17},{17,25},{25,1},{2,10},{10... | collective-permute-start | bytes 786440 | tf_op jit(solution)/shard_map/ppermute | solution.py:430
  91.0 9.3 %collective-permute-start.3 = (bf16[1024,128]{1,0:T(8,128)(2,1)S(1)}, bf16[1024,128]{1,0:T(8,128)(2,1)S(1)}, u32[]{:S(2)}, u32[]{:S(2)}) collective-permute-start(bf16[1024,128]{1,0:T(8,128)(2,1)S(1)} %get-tuple-element.31), channel_id=1, source_target_pairs={{0,24},{8,0},{16,8},{24,16},{1,25},{9,1},{17,9},{25,17},{2,26},{10... | collective-permute-start | bytes 786440 | tf_op jit(solution)/shard_map/ppermute | solution.py:430
  100.4 2.9 %copy-start = (bf16[4,1024,128]{2,1,0:T(8,128)(2,1)}, bf16[4,1024,128]{2,1,0:T(8,128)(2,1)S(1)}, u32[]{:S(2)}) copy-start(bf16[4,1024,128]{2,1,0:T(8,128)(2,1)S(1)} %pad_maximum_fusion.same_ref) | copy-start | bytes 3145732
  100.4 2.9 %collective-permute-start.4 = (bf16[4,1024,128]{2,1,0:T(8,128)(2,1)S(1)}, bf16[4,1024,128]{2,1,0:T(8,128)(2,1)S(1)}, u32[]{:S(2)}, u32[]{:S(2)}) collective-permute-start(bf16[4,1024,128]{2,1,0:T(8,128)(2,1)S(1)} %pad_maximum_fusion.same_ref), channel_id=1, source_target_pairs={{0,4},{4,0},{1,5},{5,1},{2,6},{6,2},{3,7},{7,3},{8,12},{12,8},{9,1... | collective-permute-start | bytes 3145736 | tf_op jit(solution)/shard_map/ppermute | solution.py:431
  103.4 1.1 copy-start.5
  138.5 2.9 %collective-permute-start.5 = (bf16[4,1024,128]{2,1,0:T(8,128)(2,1)}, bf16[4,1024,128]{2,1,0:T(8,128)(2,1)S(1)}, u32[]{:S(2)}, u32[]{:S(2)}) collective-permute-start(bf16[4,1024,128]{2,1,0:T(8,128)(2,1)} %get-tuple-element.17), channel_id=1, source_target_pairs={{0,4},{4,0},{1,5},{5,1},{2,6},{6,2},{3,7},{7,3},{8,12},{12,8},{9,1... | collective-permute-start | bytes 3145736 | tf_op jit(solution)/shard_map/ppermute | solution.py:446
  142.9 16.2 %copy-start.9 = (bf16[8,64,128]{2,1,0:T(8,128)(2,1)S(1)}, bf16[8,64,128]{2,1,0:T(8,128)(2,1)}, u32[]{:S(2)}) copy-start(bf16[8,64,128]{2,1,0:T(8,128)(2,1)} %get-tuple-element.18) | copy-start | bytes 393220
  143.0 9.2 %collective-permute-start.6 = (bf16[1024,128]{1,0:T(8,128)(2,1)S(1)}, bf16[1024,128]{1,0:T(8,128)(2,1)S(1)}, u32[]{:S(2)}, u32[]{:S(2)}) collective-permute-start(bf16[1024,128]{1,0:T(8,128)(2,1)S(1)} %get-tuple-element.27), channel_id=1, source_target_pairs={{0,24},{8,0},{16,8},{24,16},{1,25},{9,1},{17,9},{25,17},{2,26},{10... | collective-permute-start | bytes 786440 | tf_op jit(solution)/shard_map/ppermute | solution.py:450
  144.0 10.4 %collective-permute-start.8 = (bf16[1024,128]{1,0:T(8,128)(2,1)S(1)}, bf16[1024,128]{1,0:T(8,128)(2,1)S(1)}, u32[]{:S(2)}, u32[]{:S(2)}) collective-permute-start(bf16[1024,128]{1,0:T(8,128)(2,1)S(1)} %get-tuple-element.28), channel_id=1, source_target_pairs={{0,8},{8,16},{16,24},{24,0},{1,9},{9,17},{17,25},{25,1},{2,10},{10... | collective-permute-start | bytes 786440 | tf_op jit(solution)/shard_map/ppermute | solution.py:450
  145.1 13.8 %collective-permute-start.7 = (bf16[1024,128]{1,0:T(8,128)(2,1)S(1)}, bf16[1024,128]{1,0:T(8,128)(2,1)S(1)}, u32[]{:S(2)}, u32[]{:S(2)}) collective-permute-start(bf16[1024,128]{1,0:T(8,128)(2,1)S(1)} %get-tuple-element.29), channel_id=1, source_target_pairs={{0,16},{8,24},{16,0},{24,8},{1,17},{9,25},{17,1},{25,9},{2,18},{10... | collective-permute-start | bytes 786440 | tf_op jit(solution)/shard_map/ppermute | solution.py:450
  147.3 12.6 %all-to-all-start.1 = ((bf16[8,64,128]{2,1,0:T(8,128)(2,1)}), bf16[8,64,128]{2,1,0:T(8,128)(2,1)S(1)}, u32[]{:S(2)}, u32[]{:S(2)}) async-start(bf16[8,64,128]{2,1,0:T(8,128)(2,1)} %get-tuple-element.13), calls=%async_computation.1 | async-start | bytes 262144 | tf_op jit(solution)/shard_map/all_to_all | solution.py:434
  159.9 4.0 %copy-start.8 = (bf16[8,64,128]{2,1,0:T(8,128)(2,1)}, bf16[8,64,128]{2,1,0:T(8,128)(2,1)S(1)}, u32[]{:S(2)}) copy-start(bf16[8,64,128]{2,1,0:T(8,128)(2,1)S(1)} %all-to-all-done.1.heads_ref) | copy-start | bytes 393220
  159.9 11.8 %all-to-all-start.3 = ((bf16[8,192,128]{2,1,0:T(8,128)(2,1)}), bf16[8,192,128]{2,1,0:T(8,128)(2,1)S(1)}, u32[]{:S(2)}, u32[]{:S(2)}) async-start(bf16[8,192,128]{2,1,0:T(8,128)(2,1)} %pad_maximum_fusion.1), calls=%async_computation.3 | async-start | bytes 786432 | tf_op jit(solution)/shard_map/all_to_all | solution.py:454
  171.7 5.1 %copy-start.7 = (bf16[8,192,128]{2,1,0:T(8,128)(2,1)}, bf16[8,192,128]{2,1,0:T(8,128)(2,1)S(1)}, u32[]{:S(2)}) copy-start(bf16[8,192,128]{2,1,0:T(8,128)(2,1)S(1)} %all-to-all-done.3.back_ref) | copy-start | bytes 1179652
  171.7 18.2 %all-to-all-start.2 = ((bf16[4,128,512]{2,1,0:T(8,128)(2,1)}), bf16[4,128,512]{2,1,0:T(8,128)(2,1)S(1)}, u32[]{:S(2)}, u32[]{:S(2)}) async-start(bf16[4,128,512]{2,1,0:T(8,128)(2,1)} %get-tuple-element.14), calls=%async_computation.2 | async-start | bytes 1048576 | tf_op jit(solution)/shard_map/all_to_all | solution.py:436
  206.4 9.2 %copy-start.6 = (bf16[128,512]{1,0:T(8,128)(2,1)S(1)}, bf16[128,512]{1,0:T(8,128)(2,1)}, u32[]{:S(2)}) copy-start(bf16[128,512]{1,0:T(8,128)(2,1)} %embed.1.summed_ref) | copy-start | bytes 393220
  206.4 37.7 %all-to-all-start.5 = ((bf16[64,32,512]{2,1,0:T(8,128)(2,1)}), bf16[64,32,512]{2,1,0:T(8,128)(2,1)S(1)}, u32[]{:S(2)}, u32[]{:S(2)}) async-start(bf16[64,32,512]{2,1,0:T(8,128)(2,1)} %bitcast.37), calls=%async_computation.5 | async-start | bytes 4194304 | tf_op jit(solution)/shard_map/all_to_all | solution.py:440
  244.0 1.3 copy-start.2
